TPU v7x, 32 devices: a whole 2x2x4 slice. The times are simulated.
32 devices in a mesh: dp: 16 (over z, y, x), tensor: 2 (over core).
Axes of the slice: x: 2, y: 2, z: 4, core: 2. Of those that a mesh axis runs over, the one named last changes fastest.
Arguments:
- tokens: bfloat16 [4096, 768], P(('dp', 'tensor')), may hold values from -6 to 6
- bounds: int32 [16, 5], P('dp'), may hold values from 0 to 256, as said below
- w_qkv: bfloat16 [3, 768, 768], P(None, None, 'tensor'), may hold values from -0.21875 to 0.21875
- b_qkv: bfloat16 [3, 768], P(None, 'tensor'), may hold values from -4 to 4
- w_dense: bfloat16 [768, 768], P('tensor'), may hold values from -0.875 to 0.875
- b_dense: bfloat16 [768], replicated, may hold values from -4 to 4
- w_up: bfloat16 [768, 3072], P(None, 'tensor'), may hold values from -0.21875 to 0.21875
- b_up: bfloat16 [3072], P('tensor'), may hold values from -6 to 6
- w_down: bfloat16 [3072, 768], P('tensor'), may hold values from -0.109375 to 0.109375
- b_down: bfloat16 [768], replicated, may hold values from -4 to 4
- norm1_gain: bfloat16 [768], replicated, may hold values from 0.099609375 to 1.8984375
- norm1_shift: bfloat16 [768], replicated, may hold values from -4 to 4
- norm2_gain: bfloat16 [768], replicated, may hold values from 0.099609375 to 1.8984375
- norm2_shift: bfloat16 [768], replicated, may hold values from -4 to 4
- cotangent: bfloat16 [4096, 768], P(('dp', 'tensor')), may hold values from -6 to 6
Outputs:
- output: bfloat16 [4096, 768], P(('dp', 'tensor'))
- grad_input: bfloat16 [4096, 768], P(('dp', 'tensor'))
- grad_qkv: float32 [3, 768, 768], P(None, 'dp', 'tensor')
- grad_qkv_bias: float32 [3, 768], P(None, 'tensor')
- grad_dense: float32 [768, 768], P('tensor', 'dp')
- grad_dense_bias: float32 [768], replicated
- grad_up: float32 [768, 3072], P('dp', 'tensor')
- grad_up_bias: float32 [3072], P('tensor')
- grad_down: float32 [3072, 768], P('tensor', 'dp')
- grad_down_bias: float32 [768], replicated
- grad_norm1_gain: float32 [768], replicated
- grad_norm1_shift: float32 [768], replicated
- grad_norm2_gain: float32 [768], replicated
- grad_norm2_shift: float32 [768], replicated
Inputs may be any that keep to these rules, and one draw needn't show every extreme that they name: `bounds`: each row starts with 0 and never falls; each rise is 0 or at least 64; the first rise is at least 129; the last entry is the group's used slots, and some group uses all 256.
All inputs are finite; a program needn't handle non-finite values.
Results may differ from a plain program's by a relative error of at most 0.0095.
Values may be sent and summed in bfloat16 or wider, within the bound.
A program may use at most 128 MiB of HBM per device.

v0:
```python
import math

import jax
import jax.numpy as jnp
from jax import lax
from jax.sharding import PartitionSpec as P

D = 768
HEAD = 64
ROT = 16


EPS = 1e-05


def normalize_rows(rows, gain, shift):
    center = rows - jnp.mean(rows, -1, keepdims=True)
    spread = jnp.mean(center * center, -1, keepdims=True)
    scaler = lax.rsqrt(spread + EPS)
    normal = center * scaler
    return (normal * gain + shift, normal, scaler)


def norm_back(grad_out, normal, scaler, gain):
    scaled = grad_out * gain
    inner_mean = jnp.mean(scaled, -1, keepdims=True)
    cross_mean = jnp.mean(scaled * normal, -1, keepdims=True)
    into = scaler * (scaled - inner_mean - normal * cross_mean)
    return (into, jnp.sum(grad_out * normal, 0), jnp.sum(grad_out, 0))


def turn_half(v):
    half = ROT // 2
    return jnp.concatenate([-v[..., half:ROT], v[..., :half]], -1)


def unturn_half(v):
    half = ROT // 2
    return jnp.concatenate([v[..., half:ROT], -v[..., :half]], -1)


def rotary(v, cosine, sine):
    part = v[..., :ROT]
    return jnp.concatenate([part * cosine + turn_half(part) * sine, v[..., ROT:]], -1)


def unrotary(grad, cosine, sine):
    part = grad[..., :ROT]
    return jnp.concatenate([part * cosine + unturn_half(part * sine), grad[..., ROT:]], -1)


def layout(bounds_row, count):
    slot_count = bounds_row.shape[0]
    steps = jnp.arange(count, dtype=jnp.int32)
    segment = jnp.sum((steps[:, None] >= bounds_row[None, 1:]).astype(jnp.int32), 1)
    slot_ids = jnp.arange(slot_count, dtype=jnp.int32)
    start = jnp.sum(jnp.where(slot_ids[None, :] == segment[:, None], bounds_row[None, :], 0), 1)
    place = (steps - start).astype(jnp.float32)
    inverse = 10000.0 ** (-jnp.arange(0, ROT, 2).astype(jnp.float32) / ROT)
    angle = place[:, None] * inverse[None, :]
    angle = jnp.concatenate([angle, angle], -1)[:, None, :]
    allowed = (segment[:, None] == segment[None, :]) & (steps[None, :] <= steps[:, None])
    return (jnp.cos(angle), jnp.sin(angle), allowed)


def gelu_exact(v):
    return jax.nn.gelu(v, approximate=False)


def on_device(
    tokens,
    bounds,
    w_qkv,
    b_qkv,
    w_dense,
    b_dense,
    w_up,
    b_up,
    w_down,
    b_down,
    norm1_gain,
    norm1_shift,
    norm2_gain,
    norm2_shift,
    cotangent,
):
    f32 = jnp.float32
    bf16 = jnp.bfloat16
    scale = 1.0 / math.sqrt(HEAD)
    dp_count = lax.axis_size("dp")
    share = D // dp_count
    rows = tokens.astype(f32)
    gain_one = norm1_gain.astype(f32)
    gain_two = norm2_gain.astype(f32)
    first_own, normal_one, scaler_one = normalize_rows(rows, gain_one, norm1_shift.astype(f32))
    second_own, normal_two, scaler_two = normalize_rows(rows, gain_two, norm2_shift.astype(f32))
    first, second = (
        lax.all_gather(first_own.astype(bf16), "tensor", axis=0, tiled=True),
        lax.all_gather(second_own.astype(bf16), "tensor", axis=0, tiled=True),
    )
    count = first.shape[0]
    width = w_qkv.shape[2]
    heads = width // HEAD
    cosine, sine, allowed = layout(bounds[0], count)
    project = (
        jnp.einsum("td,cde->cte", first, w_qkv, preferred_element_type=f32)
        + b_qkv.astype(f32)[:, None, :]
    )
    split = project.reshape(3, count, heads, HEAD)
    query = rotary(split[0], cosine, sine).astype(bf16)
    key = rotary(split[1], cosine, sine).astype(bf16)
    value = split[2].astype(bf16)
    raw = jnp.einsum("qhe,khe->hqk", query, key, preferred_element_type=f32)
    scaled = jnp.where(allowed[None], raw * scale, -1e30)
    top = jnp.max(scaled, -1, keepdims=True)
    weights = jnp.exp(scaled - top)
    total = jnp.sum(weights, -1, keepdims=True)
    log_total = top + jnp.log(total)
    probs = weights / total
    mixed = jnp.einsum("hqk,khe->qhe", probs.astype(bf16), value, preferred_element_type=f32)
    mixed = mixed.astype(bf16).reshape(count, width)
    inner = jnp.dot(second, w_up, preferred_element_type=f32) + b_up.astype(f32)
    active = gelu_exact(inner).astype(bf16)
    summed = lax.psum_scatter(
        (
            jnp.dot(mixed, w_dense, preferred_element_type=f32)
            + jnp.dot(active, w_down, preferred_element_type=f32)
        ).astype(jnp.bfloat16),
        "tensor",
        scatter_dimension=0,
        tiled=True,
    ).astype(jnp.float32)
    output = (rows + summed + (b_dense.astype(f32) + b_down.astype(f32))).astype(bf16)
    back = lax.all_gather(cotangent, "tensor", axis=0, tiled=True)
    back_cut = back.reshape(count, dp_count, share)
    second_cut = second.reshape(count, dp_count, share)
    first_cut = first.reshape(count, dp_count, share)
    grad_dense_w = jnp.einsum("te,tnr->ner", mixed, back_cut, preferred_element_type=f32)
    grad_down_w = jnp.einsum("tf,tnr->nfr", active, back_cut, preferred_element_type=f32)
    grad_active = jnp.einsum("td,fd->tf", back, w_down, preferred_element_type=f32)
    grad_inner = jax.vjp(gelu_exact, inner)[1](grad_active)[0].astype(bf16)
    grad_up_w = jnp.einsum("tnr,tf->nrf", second_cut, grad_inner, preferred_element_type=f32)
    grad_up_b = jnp.sum(grad_inner.astype(f32), 0)
    part_second = jnp.einsum("tf,df->td", grad_inner, w_up, preferred_element_type=f32)
    terms_up, terms_down = (
        lax.all_to_all(
            grad_up_w.astype(jnp.bfloat16), "dp", split_axis=0, concat_axis=0, tiled=True
        ).astype(grad_up_w.dtype),
        lax.all_to_all(
            grad_down_w.astype(jnp.bfloat16), "dp", split_axis=0, concat_axis=0, tiled=True
        ).astype(grad_down_w.dtype),
    )
    shard_up = jnp.sum(terms_up, 0)
    shard_down = jnp.sum(terms_down, 0)
    grad_mixed = jnp.einsum("td,ed->te", back, w_dense, preferred_element_type=f32)
    grad_mixed = grad_mixed.astype(bf16).reshape(count, heads, HEAD)
    again = jnp.exp(scaled - log_total)
    grad_probs = jnp.einsum("qhe,khe->hqk", grad_mixed, value, preferred_element_type=f32)
    inner_sum = jnp.sum(grad_probs * again, -1, keepdims=True)
    grad_raw = (again * (grad_probs - inner_sum) * scale).astype(bf16)
    grad_query = jnp.einsum("hqk,khe->qhe", grad_raw, key, preferred_element_type=f32)
    grad_key = jnp.einsum("hqk,qhe->khe", grad_raw, query, preferred_element_type=f32)
    grad_value = jnp.einsum(
        "hqk,qhe->khe", again.astype(bf16), grad_mixed, preferred_element_type=f32
    )
    grad_project = jnp.stack(
        [unrotary(grad_query, cosine, sine), unrotary(grad_key, cosine, sine), grad_value]
    )
    grad_project = grad_project.reshape(3, count, width).astype(bf16)
    grad_qkv_w = jnp.einsum("tnr,cte->ncre", first_cut, grad_project, preferred_element_type=f32)
    grad_qkv_b = jnp.sum(grad_project.astype(f32), 1)
    part_first = jnp.einsum("cte,cde->td", grad_project, w_qkv, preferred_element_type=f32)
    terms_qkv, terms_dense = (
        lax.all_to_all(
            grad_qkv_w.astype(jnp.bfloat16), "dp", split_axis=0, concat_axis=0, tiled=True
        ).astype(grad_qkv_w.dtype),
        lax.all_to_all(
            grad_dense_w.astype(jnp.bfloat16), "dp", split_axis=0, concat_axis=0, tiled=True
        ).astype(grad_dense_w.dtype),
    )
    shard_qkv = jnp.sum(terms_qkv, 0)
    shard_dense = jnp.sum(terms_dense, 0)
    sum_qkv_b, sum_up_b = lax.psum((grad_qkv_b, grad_up_b), "dp")
    grad_first, grad_second = (
        lax.psum_scatter(
            part_first.astype(jnp.bfloat16), "tensor", scatter_dimension=0, tiled=True
        ).astype(jnp.float32),
        lax.psum_scatter(
            part_second.astype(jnp.bfloat16), "tensor", scatter_dimension=0, tiled=True
        ).astype(jnp.float32),
    )
    back_own = cotangent.astype(f32)
    into_one, gain_grad_one, shift_grad_one = norm_back(
        grad_first, normal_one, scaler_one, gain_one
    )
    into_two, gain_grad_two, shift_grad_two = norm_back(
        grad_second, normal_two, scaler_two, gain_two
    )
    grad_input = (back_own + into_one + into_two).astype(bf16)
    gain_sum_one, shift_sum_one, gain_sum_two, shift_sum_two, bias_sum = lax.psum(
        (gain_grad_one, shift_grad_one, gain_grad_two, shift_grad_two, jnp.sum(back_own, 0)),
        ("dp", "tensor"),
    )
    return (
        output,
        grad_input,
        shard_qkv,
        sum_qkv_b,
        shard_dense,
        bias_sum,
        shard_up,
        sum_up_b,
        shard_down,
        bias_sum,
        gain_sum_one,
        shift_sum_one,
        gain_sum_two,
        shift_sum_two,
    )


def solution(mesh):
    return jax.shard_map(
        on_device,
        mesh=mesh,
        in_specs=(
            P(("dp", "tensor"), None),
            P("dp", None),
            P(None, None, "tensor"),
            P(None, "tensor"),
            P("tensor", None),
            P(),
            P(None, "tensor"),
            P("tensor"),
            P("tensor", None),
            P(),
            P(),
            P(),
            P(),
            P(),
            P(("dp", "tensor"), None),
        ),
        out_specs=(
            P(("dp", "tensor"), None),
            P(("dp", "tensor"), None),
            P(None, "dp", "tensor"),
            P(None, "tensor"),
            P("tensor", "dp"),
            P(),
            P("dp", "tensor"),
            P("tensor"),
            P("tensor", "dp"),
            P(),
            P(),
            P(),
            P(),
            P(),
        ),
        check_vma=False,
    )
```

profile of v0, /device:TPU:0, one launch (start us, length us, event | category | flops | bytes accessed | tf_op | source)
XLA Modules:
  0.0 353.5 jit_solution(9532821541123140554)
XLA Ops:
  7.2 1.2 convert_reduce_fusion.8
  8.4 1.1 fusion.59
  9.6 0.7 convert_element_type.148
  10.3 0.7 convert_element_type.159
  10.9 0.7 convert_element_type.149
  11.6 0.7 convert_element_type.160
  12.3 0.7 convert_element_type.151
  13.0 1.8 fusion.50
  14.8 2.2 all_gather.9
  17.0 2.2 fusion.16
  19.2 0.7 slice.136
  19.9 0.9 copy.84
  20.8 1.6 slice.140
  22.6 0.7 slice.139
  23.3 1.5 slice_negate_fusion.2
  25.0 0.7 fusion.67
  26.5 2.3 all_gather.11
  28.8 1.7 copy.83
  30.6 1.0 fusion.71
  32.2 1.5 fusion.87
  35.2 0.9 convert_bitcast_fusion.2
  36.1 8.3 %all-to-all-start.1 = ((bf16[16,384,48]{1,2,0:T(8,128)(2,1)}), bf16[16,384,48]{1,2,0:T(8,128)(2,1)}, u32[]{:S(2)}, u32[]{:S(2)}) async-start(bf16[16,384,48]{1,2,0:T(8,128)(2,1)} %convert_bitcast_fusion.2), calls=%async_computation.4 | async-start | bytes 1179648 | tf_op jit(solution)/shard_map/all_to_all | solution.py:177
  44.6 1.3 log_add_fusion
  45.9 1.4 convolution_convert_fusion.3
  47.5 2.6 fusion.89
  50.5 4.5 %fusion.20 = f32[256,6,64]{0,2,1:T(8,128)} fusion(f32[6,256,256]{1,2,0:T(8,128)} %fusion.89, f32[6,256,256]{1,2,0:T(8,128)} %copy-done.1, f32[6,256]{1,0:T(8,128)} %log_add_fusion, bf16[256,6,48]{0,2,1:T(8,128)(2,1)} %slice.139, bf16[256,6,16]{0,2,1:T(8,128)(2,1)} %copy-done.25), kind=kOutput, calls=%fused_computation.43 | convolution fusion | flops 53479168 | bytes 3741696 | tf_op jit(solution)/shard_map/hqk,khe->qhe/dot_general | solution.py:161
  55.0 4.4 %fusion.23 = f32[256,6,64]{0,2,1:T(8,128)} fusion(f32[6,256,256]{1,2,0:T(8,128)} %fusion.89, f32[6,256,256]{1,2,0:T(8,128)} %copy-done.1, f32[6,256]{1,0:T(8,128)S(1)} %copy-done.28, bf16[256,6,48]{0,2,1:T(8,128)(2,1)S(1)} %copy-done.19, bf16[256,6,16]{0,2,1:T(8,128)(2,1)} %copy-done.24), kind=kOutput, calls=%fused_computation.44 | convolution fusion | flops 53479168 | bytes 3741696 | tf_op jit(solution)/shard_map/hqk,qhe->khe/dot_general | solution.py:162
  59.5 1.6 slice.137
  61.1 1.6 slice.138
  62.7 1.6 slice_multiply_fusion.3
  64.5 0.9 fusion.85
  65.4 0.8 fusion.86
  66.3 1.6 fusion.72
  67.9 1.6 pad_maximum_fusion.3
  69.5 1.1 copy.91
  70.6 1.7 pad_maximum_fusion.4
  72.3 1.7 copy.92
  74.0 1.6 convert_bitcast_fusion.1
  75.6 1.4 copy.95
  77.0 7.0 %all-to-all-start = ((bf16[16,3,48,384]{3,2,1,0:T(8,128)(2,1)}), bf16[16,3,48,384]{3,2,1,0:T(8,128)(2,1)}, u32[]{:S(2)}, u32[]{:S(2)}) async-start(bf16[16,3,48,384]{3,2,1,0:T(8,128)(2,1)} %copy.95), calls=%async_computation.3 | async-start | bytes 3538944 | tf_op jit(solution)/shard_map/all_to_all | solution.py:174
  84.1 2.1 all_gather.10
  86.4 2.4 convolution_add_fusion
  88.8 5.3 %convert_reduce_fusion.3 = (f32[1536]{0:T(1024)S(1)}, bf16[256,1536]{1,0:T(8,128)(2,1)S(1)}, f32[256,1536]{1,0:T(8,128)}) fusion(f32[256,1536]{1,0:T(8,128)S(1)} %convolution_add_fusion, bf16[256,768]{1,0:T(8,128)(2,1)S(1)} %all_gather.11, bf16[1536,768]{1,0:T(8,128)(2,1)S(1)} %copy-done), kind=kOutput, calls=%fused_computation.10 | convolution fusion | flops 633076224 | bytes 6690816 | tf_op jit(solution)/shard_map/td,fd->tf/dot_general | solution.py:140
  94.2 0.9 copy-done.12
  95.1 2.2 convolution_convert_fusion
  97.3 24.2 %all-to-all-done = bf16[16,3,48,384]{3,2,1,0:T(8,128)(2,1)} async-done(((bf16[16,3,48,384]{3,2,1,0:T(8,128)(2,1)}), bf16[16,3,48,384]{3,2,1,0:T(8,128)(2,1)}, u32[]{:S(2)}, u32[]{:S(2)}) %all-to-all-start) | async-done | bytes 1769504 | tf_op jit(solution)/shard_map/all_to_all | solution.py:174
  121.5 8.4 %all-to-all-start.2 = ((bf16[16,48,1536]{2,1,0:T(8,128)(2,1)}), bf16[16,48,1536]{2,1,0:T(8,128)(2,1)}, u32[]{:S(2)}, u32[]{:S(2)}) async-start(bf16[16,48,1536]{2,1,0:T(8,128)(2,1)} %convolution_convert_fusion), calls=%async_computation.5 | async-start | bytes 4718592 | tf_op jit(solution)/shard_map/all_to_all | solution.py:146
  129.9 2.1 multiply_convert_fusion.1
  132.0 0.8 fusion.91
  132.8 1.7 convert_bitcast_fusion
  134.6 42.3 %all-to-all-done.2 = bf16[16,48,1536]{2,1,0:T(8,128)(2,1)} async-done(((bf16[16,48,1536]{2,1,0:T(8,128)(2,1)}), bf16[16,48,1536]{2,1,0:T(8,128)(2,1)}, u32[]{:S(2)}, u32[]{:S(2)}) %all-to-all-start.2) | async-done | bytes 2359328 | tf_op jit(solution)/shard_map/all_to_all | solution.py:146
  176.9 10.7 %all-to-all-start.3 = ((bf16[16,1536,48]{1,2,0:T(8,128)(2,1)}), bf16[16,1536,48]{1,2,0:T(8,128)(2,1)}, u32[]{:S(2)}, u32[]{:S(2)}) async-start(bf16[16,1536,48]{1,2,0:T(8,128)(2,1)} %convert_bitcast_fusion), calls=%async_computation.6 | async-start | bytes 4718592 | tf_op jit(solution)/shard_map/all_to_all | solution.py:149
  187.7 3.1 fusion.18
  190.8 3.5 convolution_convert_fusion.1
  194.4 0.8 fusion.88
  195.6 1.1 fusion.19
  196.9 98.5 %all-reduce.1 = (f32[3,384]{1,0:T(4,128)}, f32[1536]{0:T(1024)}) all-reduce(f32[3,384]{1,0:T(4,128)S(1)} %convert_reduce_fusion.5, f32[1536]{0:T(1024)S(1)} %get-tuple-element.32), channel_id=1, replica_groups=mesh['dp'=16,'tensor'=2] {'dp'}, use_global_device_ids=true, to_apply=%region_16.17 | all-reduce | flops 2688 | bytes 21504 | tf_op jit(solution)/shard_map/psum | solution.py:183
  295.5 1.4 fusion.65
  297.0 2.1 convert_reduce_fusion.9
  299.1 37.6 %all-reduce = (f32[768]{0:T(1024)S(1)}, f32[768]{0:T(1024)}, f32[768]{0:T(1024)}, f32[768]{0:T(1024)}, f32[768]{0:T(1024)}) all-reduce(f32[768]{0:T(1024)S(1)} %get-tuple-element.43, f32[768]{0:T(1024)S(1)} %get-tuple-element.22, f32[768]{0:T(1024)S(1)} %get-tuple-element.23, ...), channel_id=1, replica_groups=mesh['dp'=16,'tensor'=2] {'dp','tensor'}, use_global_device_ids=true, to_apply=%region_19.20 | all-reduce | flops 3840 | bytes 30720 | tf_op jit(solution)/shard_map/psum | solution.py:200
  336.8 1.8 convert_reduce_fusion.4
  338.5 2.4 convert_reduce_fusion.2
  341.0 2.7 convert_reduce_fusion.1
  343.7 2.7 convert_reduce_fusion
  (115 shorter events, 5.8 us)
Async XLA Ops:
  7.2 81.6 %copy-start = (bf16[1536,768]{1,0:T(8,128)(2,1)S(1)}, bf16[1536,768]{1,0:T(8,128)(2,1)}, u32[]{:S(2)}) copy-start(bf16[1536,768]{1,0:T(8,128)(2,1)} %param.23) | copy-start | bytes 7077892
  8.4 6.4 %copy-start.30 = (f32[128]{0:T(128)}, f32[128]{0:T(128)S(1)}, u32[]{:S(2)}) copy-start(f32[128]{0:T(128)S(1)} %broadcast_multiply_fusion.5) | copy-start | bytes 1540
  9.6 5.3 %copy-start.32 = (f32[128]{0:T(128)}, f32[128]{0:T(128)S(1)}, u32[]{:S(2)}) copy-start(f32[128]{0:T(128)S(1)} %add_rsqrt_fusion) | copy-start | bytes 1540
  10.3 4.6 %copy-start.20 = (f32[768]{0:T(1024)}, f32[768]{0:T(1024)S(1)}, u32[]{:S(2)}) copy-start(f32[768]{0:T(1024)S(1)} %convert_element_type.148) | copy-start | bytes 9220
  10.9 3.9 %copy-start.22 = (f32[768]{0:T(1024)}, f32[768]{0:T(1024)S(1)}, u32[]{:S(2)}) copy-start(f32[768]{0:T(1024)S(1)} %convert_element_type.159) | copy-start | bytes 9220
  19.9 4.9 %copy-start.38 = (s32[1,5]{1,0:T(1,128)S(1)}, s32[1,5]{1,0:T(1,128)}, u32[]{:S(2)}) copy-start(s32[1,5]{1,0:T(1,128)} %param.16) | copy-start | bytes 64
  31.5 0.6 copy-start.24
  31.6 2.1 copy-start.25
  32.2 1.7 copy-start.17
  33.6 1.2 copy-start.1
  33.7 1.1 copy-start.26
  33.9 0.9 copy-start.29
  34.8 1.3 copy-start.15
  36.1 40.9 %all-to-all-start.1 = ((bf16[16,384,48]{1,2,0:T(8,128)(2,1)}), bf16[16,384,48]{1,2,0:T(8,128)(2,1)}, u32[]{:S(2)}, u32[]{:S(2)}) async-start(bf16[16,384,48]{1,2,0:T(8,128)(2,1)} %convert_bitcast_fusion.2), calls=%async_computation.4 | async-start | bytes 1179648 | tf_op jit(solution)/shard_map/all_to_all | solution.py:177
  47.5 2.6 copy-start.2
  47.5 2.6 copy-start.27
  50.5 4.5 %copy-start.19 = (bf16[256,6,48]{0,2,1:T(8,128)(2,1)S(1)}, bf16[256,6,48]{0,2,1:T(8,128)(2,1)}, u32[]{:S(2)}) copy-start(bf16[256,6,48]{0,2,1:T(8,128)(2,1)} %slice.140) | copy-start | bytes 442372
  50.5 4.5 %copy-start.28 = (f32[6,256]{1,0:T(8,128)S(1)}, f32[6,256]{1,0:T(8,128)}, u32[]{:S(2)}) copy-start(f32[6,256]{1,0:T(8,128)} %log_add_fusion) | copy-start | bytes 18436
  55.0 7.7 %copy-start.18 = (f32[256,16]{0,1:T(8,128)S(1)}, f32[256,16]{0,1:T(8,128)}, u32[]{:S(2)}) copy-start(f32[256,16]{0,1:T(8,128)} %get-tuple-element.57) | copy-start | bytes 49156
  64.5 11.1 %copy-start.5 = (bf16[1,256,384]{2,1,0:T(8,128)(2,1)}, bf16[1,256,384]{2,1,0:T(8,128)(2,1)S(1)}, u32[]{:S(2)}) copy-start(bf16[1,256,384]{2,1,0:T(8,128)(2,1)S(1)} %copy.93) | copy-start | bytes 589828
  70.6 5.1 %copy-start.7 = (bf16[1,256,384]{2,1,0:T(8,128)(2,1)}, bf16[1,256,384]{2,1,0:T(8,128)(2,1)S(1)}, u32[]{:S(2)}) copy-start(bf16[1,256,384]{2,1,0:T(8,128)(2,1)S(1)} %copy.91) | copy-start | bytes 589828
  77.0 7.1 %copy-start.34 = (bf16[1536]{0:T(1024)(128)(2,1)S(1)}, bf16[1536]{0:T(1024)(128)(2,1)}, u32[]{:S(2)}) copy-start(bf16[1536]{0:T(1024)(128)(2,1)} %param.22) | copy-start | bytes 9220
  77.0 7.1 %copy-start.14 = (bf16[128,768]{1,0:T(8,128)(2,1)S(1)}, bf16[128,768]{1,0:T(8,128)(2,1)}, u32[]{:S(2)}) copy-start(bf16[128,768]{1,0:T(8,128)(2,1)} %get-tuple-element.42) | copy-start | bytes 589828
  77.0 44.5 %all-to-all-start = ((bf16[16,3,48,384]{3,2,1,0:T(8,128)(2,1)}), bf16[16,3,48,384]{3,2,1,0:T(8,128)(2,1)}, u32[]{:S(2)}, u32[]{:S(2)}) async-start(bf16[16,3,48,384]{3,2,1,0:T(8,128)(2,1)} %copy.95), calls=%async_computation.3 | async-start | bytes 3538944 | tf_op jit(solution)/shard_map/all_to_all | solution.py:174
  88.8 5.3 %copy-start.11 = (f32[256,1536]{1,0:T(8,128)}, f32[256,1536]{1,0:T(8,128)S(1)}, u32[]{:S(2)}) copy-start(f32[256,1536]{1,0:T(8,128)S(1)} %convolution_add_fusion) | copy-start | bytes 4718596
  94.2 0.9 copy-start.12
  121.5 55.4 %all-to-all-start.2 = ((bf16[16,48,1536]{2,1,0:T(8,128)(2,1)}), bf16[16,48,1536]{2,1,0:T(8,128)(2,1)}, u32[]{:S(2)}, u32[]{:S(2)}) async-start(bf16[16,48,1536]{2,1,0:T(8,128)(2,1)} %convolution_convert_fusion), calls=%async_computation.5 | async-start | bytes 4718592 | tf_op jit(solution)/shard_map/all_to_all | solution.py:146
  134.6 53.1 %copy-start.6 = (bf16[1,256,384]{2,1,0:T(8,128)(2,1)S(1)}, bf16[1,256,384]{2,1,0:T(8,128)(2,1)}, u32[]{:S(2)}) copy-start(bf16[1,256,384]{2,1,0:T(8,128)(2,1)} %copy-done.5) | copy-start | bytes 589828
  134.6 53.1 %copy-start.8 = (bf16[1,256,384]{2,1,0:T(8,128)(2,1)S(1)}, bf16[1,256,384]{2,1,0:T(8,128)(2,1)}, u32[]{:S(2)}) copy-start(bf16[1,256,384]{2,1,0:T(8,128)(2,1)} %copy-done.7) | copy-start | bytes 589828
  176.9 166.8 %all-to-all-start.3 = ((bf16[16,1536,48]{1,2,0:T(8,128)(2,1)}), bf16[16,1536,48]{1,2,0:T(8,128)(2,1)}, u32[]{:S(2)}, u32[]{:S(2)}) async-start(bf16[16,1536,48]{1,2,0:T(8,128)(2,1)} %convert_bitcast_fusion), calls=%async_computation.6 | async-start | bytes 4718592 | tf_op jit(solution)/shard_map/all_to_all | solution.py:149
  187.6 107.8 %reduce-scatter.6.cloned.1.call-start = ((), (), s32[]{:S(2)}) async-start(), calls=%async_computation.8 | async-start | bytes 589824 | tf_op jit(solution)/shard_map/reduce_scatter | solution.py:185
  190.8 104.6 %reduce-scatter.8.cloned.1.call-start = ((), (), s32[]{:S(2)}) async-start(), calls=%async_computation.9 | async-start | bytes 589824 | tf_op jit(solution)/shard_map/reduce_scatter | solution.py:188
  194.4 102.6 %reduce-scatter.4.cloned.1.call-start = ((), (), s32[]{:S(2)}) async-start(), calls=%async_computation.7 | async-start | bytes 589824 | tf_op jit(solution)/shard_map/reduce_scatter | solution.py:124
  194.4 1.1 copy-start.4
  194.4 1.1 copy-start.16
  195.5 1.2 copy-start.9
  195.5 1.3 copy-start.10
  195.5 99.8 %copy-start.36 = (bf16[768]{0:T(1024)(128)(2,1)S(1)}, bf16[768]{0:T(1024)(128)(2,1)}, u32[]{:S(2)}) copy-start(bf16[768]{0:T(1024)(128)(2,1)} %param.24) | copy-start | bytes 4612
  195.5 99.8 %copy-start.37 = (bf16[768]{0:T(1024)(128)(2,1)S(1)}, bf16[768]{0:T(1024)(128)(2,1)}, u32[]{:S(2)}) copy-start(bf16[768]{0:T(1024)(128)(2,1)} %param.20) | copy-start | bytes 4612
  195.5 99.9 %copy-start.3 = (bf16[128,768]{1,0:T(8,128)(2,1)S(1)}, bf16[128,768]{1,0:T(8,128)(2,1)}, u32[]{:S(2)}) copy-start(bf16[128,768]{1,0:T(8,128)(2,1)} %param.15) | copy-start | bytes 589828
  195.6 99.9 %copy-start.21 = (f32[768]{0:T(1024)S(1)}, f32[768]{0:T(1024)}, u32[]{:S(2)}) copy-start(f32[768]{0:T(1024)} %copy-done.20) | copy-start | bytes 9220
  195.6 99.9 %copy-start.23 = (f32[768]{0:T(1024)S(1)}, f32[768]{0:T(1024)}, u32[]{:S(2)}) copy-start(f32[768]{0:T(1024)} %copy-done.22) | copy-start | bytes 9220
  195.6 99.9 %copy-start.31 = (f32[128]{0:T(128)S(1)}, f32[128]{0:T(128)}, u32[]{:S(2)}) copy-start(f32[128]{0:T(128)} %copy-done.30) | copy-start | bytes 1540
  195.6 99.9 %copy-start.33 = (f32[128]{0:T(128)S(1)}, f32[128]{0:T(128)}, u32[]{:S(2)}) copy-start(f32[128]{0:T(128)} %copy-done.32) | copy-start | bytes 1540
  195.6 101.4 %copy-start.13 = (bf16[128,768]{1,0:T(8,128)(2,1)S(1)}, bf16[128,768]{1,0:T(8,128)(2,1)}, u32[]{:S(2)}) copy-start(bf16[128,768]{1,0:T(8,128)(2,1)} %param.29) | copy-start | bytes 589828
  336.7 9.7 %copy-start.35 = (f32[768]{0:T(1024)}, f32[768]{0:T(1024)S(1)}, u32[]{:S(2)}) copy-start(f32[768]{0:T(1024)S(1)} %get-tuple-element.85) | copy-start | bytes 9220
Sparse Core Ops, SparseCore 0:
  190.9 9.0 reduce-scatter.5
  202.3 8.9 reduce-scatter.7
  213.5 8.9 reduce-scatter.3
where the time goes:
time: 356 us; the launch traced here: 354 us
  blocking collectives  143 us (40%)
  waiting for transfers between devices  66.7 us (19%)
  other arithmetic  39.6 us (11%)
  matrix products  38.7 us (11%)
  starting transfers between devices  34.5 us (10%)
  local copies, waits for them, and re-layouts  17.1 us (5%)
  between operations  14.4 us (4%)
    psum x1, blocking collectives, on_device(): sum_qkv_b, sum_up_b = lax.psum((grad_qkv_b, grad_up_b), 'dp')  98.5 us
    all_to_all x1, waiting for transfers between devices, on_device(): lax.all_to_all(grad_up_w.astype(jnp.bfloat16), 'dp', split_axis=0, concat...  42.3 us
    psum x1, blocking collectives, on_device(): lax.psum((gain_grad_one, shift_grad_one, gain_grad_two, shift_grad_two, j...  37.6 us
    all_to_all x1, waiting for transfers between devices, on_device(): lax.all_to_all(grad_qkv_w.astype(jnp.bfloat16), 'dp', split_axis=0, conca...  24.2 us
    all_to_all x1, starting transfers between devices, on_device(): lax.all_to_all(grad_down_w.astype(jnp.bfloat16), 'dp', split_axis=0, conc...  10.7 us
    all_to_all x1, starting transfers between devices, on_device(): lax.all_to_all(grad_up_w.astype(jnp.bfloat16), 'dp', split_axis=0, concat...  8.38 us
    all_to_all x1, starting transfers between devices, on_device(): lax.all_to_all(grad_dense_w.astype(jnp.bfloat16), 'dp', split_axis=0, con...  8.28 us
  transfers between devices with their start and end apart: 7, of which 2 were waited for; matrix products, arithmetic and copies ran while one was open for 19% of the time, Pallas kernels for 0%

commit v1 on v0

--- a/solution.py
+++ b/solution.py
@@ -1,9 +1,18 @@
+import functools
 import math
 
 import jax
 import jax.numpy as jnp
 from jax import lax
+from jax.experimental import pallas as pl
+from jax.experimental.pallas import tpu as pltpu
 from jax.sharding import PartitionSpec as P
+
+MESH = pl.DeviceIdType.MESH
+WIDE = 128
+LAG = 2
+ROWS_DP = 24
+ROWS_ALL = 32
 
 D = 768
 HEAD = 64
@@ -65,6 +74,208 @@
 
 def gelu_exact(v):
     return jax.nn.gelu(v, approximate=False)
+
+
+def bit_orders(steps):
+    plain = list(range(steps))
+    other = [1, 0] + plain[2:] if steps > 1 else plain
+    return plain, other
+
+
+def place_rows(left, dp_count, share, padded, order):
+    count = left.shape[0]
+    steps = len(order)
+    rows = left.T.reshape(dp_count, share, count)
+    if padded != share:
+        rows = jnp.pad(rows, ((0, 0), (0, padded - share), (0, 0)))
+    rows = rows.reshape((2,) * steps + (padded, count))
+    rows = rows.transpose([steps - 1 - b for b in order] + [steps, steps + 1])
+    return rows.reshape(dp_count * padded, count)
+
+
+def reduce_kernel(plan, orders, dp_count, padded, *refs):
+    lefts, rights = refs[:6], refs[6:10]
+    vec_ref, out_ref, vec_out = refs[10:13]
+    grid, landed, vec_acc, vec_got = refs[13:17]
+    send_sem, recv_sem, vec_send, vec_recv = refs[17:]
+    steps = len(orders[0])
+    me = lax.axis_index("dp")
+    side = lax.axis_index("tensor")
+    bits = [(me // (1 << b)) % 2 for b in range(steps)]
+    mates = [me + (1 - 2 * bits[b]) * (1 << b) for b in range(steps)]
+
+    barrier = pltpu.get_barrier_semaphore()
+    for mate in mates:
+        pl.semaphore_signal(barrier, inc=1, device_id=(mate, side), device_id_type=MESH)
+    pl.semaphore_signal(barrier, inc=1, device_id=(me, 1 - side), device_id_type=MESH)
+    pl.semaphore_wait(barrier, steps + 1)
+
+    def span(chunk, step):
+        order = orders[chunk % 2]
+        start = 0
+        for s in range(step):
+            start = start + bits[order[s]] * ((dp_count >> (s + 1)) * padded)
+        return start, (dp_count >> (step + 1)) * padded
+
+    def copy(chunk, step):
+        order = orders[chunk % 2]
+        start, half = span(chunk, step)
+        away = pl.multiple_of(start + (1 - bits[order[step]]) * half, 16)
+        offset = (dp_count - (dp_count >> step)) * padded
+        return pltpu.make_async_remote_copy(
+            src_ref=grid.at[chunk, pl.ds(away, half)],
+            dst_ref=landed.at[chunk, pl.ds(offset, half)],
+            send_sem=send_sem.at[chunk, step],
+            recv_sem=recv_sem.at[chunk, step],
+            device_id=(mates[order[step]], side),
+            device_id_type=MESH,
+        )
+
+    def absorb(chunk, step):
+        order = orders[chunk % 2]
+        start, half = span(chunk, step)
+        copy(chunk, step).wait_recv()
+        keep = pl.ds(pl.multiple_of(start + bits[order[step]] * half, 16), half)
+        offset = (dp_count - (dp_count >> step)) * padded
+        total = grid[chunk, keep].astype(jnp.float32) + landed[chunk, pl.ds(offset, half)].astype(
+            jnp.float32
+        )
+        if step == steps - 1:
+            out_ref[chunk] = total
+        else:
+            grid[chunk, keep] = total.astype(jnp.bfloat16)
+
+    def produce(chunk):
+        which, right, column = plan[chunk]
+        grid[chunk] = jnp.dot(
+            lefts[2 * which + chunk % 2][...],
+            rights[right][:, pl.ds(column, WIDE)],
+            preferred_element_type=jnp.float32,
+        ).astype(jnp.bfloat16)
+
+    def vec_copy(step):
+        if step == 0:
+            rows, target = pl.ds(ROWS_DP, ROWS_ALL), (me, 1 - side)
+        else:
+            rows, target = pl.ds(0, ROWS_DP + ROWS_ALL), (mates[step - 1], side)
+        return pltpu.make_async_remote_copy(
+            src_ref=vec_acc.at[step, rows],
+            dst_ref=vec_got.at[step, rows],
+            send_sem=vec_send.at[step],
+            recv_sem=vec_recv.at[step],
+            device_id=target,
+            device_id_type=MESH,
+        )
+
+    def vec_step(step):
+        if step == 0:
+            vec_acc[0] = vec_ref[...]
+        else:
+            vec_copy(step - 1).wait_recv()
+            if step == 1:
+                vec_acc[1, :ROWS_DP] = vec_acc[0, :ROWS_DP]
+                vec_acc[1, ROWS_DP:] = vec_acc[0, ROWS_DP:] + vec_got[0, ROWS_DP:]
+            elif step <= steps:
+                vec_acc[step] = vec_acc[step - 1] + vec_got[step - 1]
+            else:
+                vec_out[...] = vec_acc[step - 1] + vec_got[step - 1]
+        if step <= steps:
+            vec_copy(step).start()
+
+    chunks = len(plan)
+    ticks = chunks + LAG * steps
+    for tick in range(ticks):
+        for step in range(steps, -1, -1):
+            chunk = tick - LAG * step
+            if 0 <= chunk < chunks:
+                if step > 0:
+                    absorb(chunk, step - 1)
+                else:
+                    produce(chunk)
+                if step < steps:
+                    copy(chunk, step).start()
+        if tick % 3 == 0 and tick // 3 <= steps + 1:
+            vec_step(tick // 3)
+    for chunk in range(chunks):
+        for step in range(steps):
+            copy(chunk, step).wait_send()
+    for step in range(steps + 1):
+        vec_copy(step).wait_send()
+
+
+def reduce_grads(first, second, back, grad_project, mixed, grad_inner, active, vec_dp, vec_all):
+    f32 = jnp.float32
+    bf16 = jnp.bfloat16
+    dp_count = lax.axis_size("dp")
+    steps = dp_count.bit_length() - 1
+    share = D // dp_count
+    padded = -(-share // 16) * 16
+    orders = bit_orders(steps)
+    lefts = [
+        place_rows(left, dp_count, share, padded, order)
+        for left in (second, back, first)
+        for order in orders
+    ]
+    rights = (grad_inner, active, grad_project, mixed)
+    plan = []
+    for which, right in ((0, 0), (1, 1), (2, 2), (1, 3)):
+        plan += [(which, right, c) for c in range(0, rights[right].shape[1], WIDE)]
+    flat_dp = jnp.concatenate([v.reshape(-1) for v in vec_dp])
+    flat_all = jnp.concatenate([v.reshape(-1) for v in vec_all])
+    vec = jnp.concatenate(
+        [
+            jnp.pad(flat_dp, (0, ROWS_DP * 128 - flat_dp.shape[0])),
+            jnp.pad(flat_all, (0, ROWS_ALL * 128 - flat_all.shape[0])),
+        ]
+    ).reshape(ROWS_DP + ROWS_ALL, 128)
+    chunks = len(plan)
+    whole = pl.BlockSpec(memory_space=pltpu.VMEM)
+    out, vec = pl.pallas_call(
+        functools.partial(reduce_kernel, plan, orders, dp_count, padded),
+        out_shape=(
+            jax.ShapeDtypeStruct((chunks, padded, WIDE), f32),
+            jax.ShapeDtypeStruct((ROWS_DP + ROWS_ALL, 128), f32),
+        ),
+        in_specs=[whole] * 11,
+        out_specs=(whole, whole),
+        scratch_shapes=[
+            pltpu.VMEM((chunks, dp_count * padded, WIDE), bf16),
+            pltpu.VMEM((chunks, (dp_count - 1) * padded, WIDE), bf16),
+            pltpu.VMEM((steps + 1, ROWS_DP + ROWS_ALL, 128), f32),
+            pltpu.VMEM((steps + 1, ROWS_DP + ROWS_ALL, 128), f32),
+            pltpu.SemaphoreType.DMA((chunks, steps)),
+            pltpu.SemaphoreType.DMA((chunks, steps)),
+            pltpu.SemaphoreType.DMA((steps + 1,)),
+            pltpu.SemaphoreType.DMA((steps + 1,)),
+        ],
+        compiler_params=pltpu.CompilerParams(
+            collective_id=0, has_side_effects=True, vmem_limit_bytes=60 * 1024 * 1024
+        ),
+    )(*lefts, *rights, vec)
+    out = out[:, :share]
+    pieces = []
+    at = 0
+    for right in rights:
+        number = right.shape[1] // WIDE
+        pieces.append(out[at : at + number])
+        at += number
+    up, down, qkv, dense = pieces
+    shard_up = up.transpose(1, 0, 2).reshape(share, -1)
+    shard_down = down.transpose(0, 2, 1).reshape(-1, share)
+    shard_dense = dense.transpose(0, 2, 1).reshape(-1, share)
+    each = qkv.shape[0] // 3
+    shard_qkv = qkv.reshape(3, each, share, WIDE).transpose(0, 2, 1, 3).reshape(3, share, -1)
+    flat = vec.reshape(-1)
+    results = []
+    at = 0
+    for v in vec_dp:
+        results.append(flat[at : at + v.size].reshape(v.shape))
+        at += v.size
+    at = ROWS_DP * 128
+    for v in vec_all:
+        results.append(flat[at : at + v.size].reshape(v.shape))
+        at += v.size
+    return shard_up, shard_down, shard_qkv, shard_dense, results
 
 
 def on_device(
@@ -87,8 +298,6 @@
     f32 = jnp.float32
     bf16 = jnp.bfloat16
     scale = 1.0 / math.sqrt(HEAD)
-    dp_count = lax.axis_size("dp")
-    share = D // dp_count
     rows = tokens.astype(f32)
     gain_one = norm1_gain.astype(f32)
     gain_two = norm2_gain.astype(f32)
@@ -132,26 +341,10 @@
     ).astype(jnp.float32)
     output = (rows + summed + (b_dense.astype(f32) + b_down.astype(f32))).astype(bf16)
     back = lax.all_gather(cotangent, "tensor", axis=0, tiled=True)
-    back_cut = back.reshape(count, dp_count, share)
-    second_cut = second.reshape(count, dp_count, share)
-    first_cut = first.reshape(count, dp_count, share)
-    grad_dense_w = jnp.einsum("te,tnr->ner", mixed, back_cut, preferred_element_type=f32)
-    grad_down_w = jnp.einsum("tf,tnr->nfr", active, back_cut, preferred_element_type=f32)
     grad_active = jnp.einsum("td,fd->tf", back, w_down, preferred_element_type=f32)
     grad_inner = jax.vjp(gelu_exact, inner)[1](grad_active)[0].astype(bf16)
-    grad_up_w = jnp.einsum("tnr,tf->nrf", second_cut, grad_inner, preferred_element_type=f32)
     grad_up_b = jnp.sum(grad_inner.astype(f32), 0)
     part_second = jnp.einsum("tf,df->td", grad_inner, w_up, preferred_element_type=f32)
-    terms_up, terms_down = (
-        lax.all_to_all(
-            grad_up_w.astype(jnp.bfloat16), "dp", split_axis=0, concat_axis=0, tiled=True
-        ).astype(grad_up_w.dtype),
-        lax.all_to_all(
-            grad_down_w.astype(jnp.bfloat16), "dp", split_axis=0, concat_axis=0, tiled=True
-        ).astype(grad_down_w.dtype),
-    )
-    shard_up = jnp.sum(terms_up, 0)
-    shard_down = jnp.sum(terms_down, 0)
     grad_mixed = jnp.einsum("td,ed->te", back, w_dense, preferred_element_type=f32)
     grad_mixed = grad_mixed.astype(bf16).reshape(count, heads, HEAD)
     again = jnp.exp(scaled - log_total)
@@ -167,20 +360,8 @@
         [unrotary(grad_query, cosine, sine), unrotary(grad_key, cosine, sine), grad_value]
     )
     grad_project = grad_project.reshape(3, count, width).astype(bf16)
-    grad_qkv_w = jnp.einsum("tnr,cte->ncre", first_cut, grad_project, preferred_element_type=f32)
     grad_qkv_b = jnp.sum(grad_project.astype(f32), 1)
     part_first = jnp.einsum("cte,cde->td", grad_project, w_qkv, preferred_element_type=f32)
-    terms_qkv, terms_dense = (
-        lax.all_to_all(
-            grad_qkv_w.astype(jnp.bfloat16), "dp", split_axis=0, concat_axis=0, tiled=True
-        ).astype(grad_qkv_w.dtype),
-        lax.all_to_all(
-            grad_dense_w.astype(jnp.bfloat16), "dp", split_axis=0, concat_axis=0, tiled=True
-        ).astype(grad_dense_w.dtype),
-    )
-    shard_qkv = jnp.sum(terms_qkv, 0)
-    shard_dense = jnp.sum(terms_dense, 0)
-    sum_qkv_b, sum_up_b = lax.psum((grad_qkv_b, grad_up_b), "dp")
     grad_first, grad_second = (
         lax.psum_scatter(
             part_first.astype(jnp.bfloat16), "tensor", scatter_dimension=0, tiled=True
@@ -197,10 +378,19 @@
         grad_second, normal_two, scaler_two, gain_two
     )
     grad_input = (back_own + into_one + into_two).astype(bf16)
-    gain_sum_one, shift_sum_one, gain_sum_two, shift_sum_two, bias_sum = lax.psum(
+    shard_up, shard_down, shard_qkv, shard_dense, vectors = reduce_grads(
+        first,
+        second,
+        back,
+        grad_project.transpose(1, 0, 2).reshape(count, 3 * width),
+        mixed,
+        grad_inner,
+        active,
+        (grad_qkv_b, grad_up_b),
         (gain_grad_one, shift_grad_one, gain_grad_two, shift_grad_two, jnp.sum(back_own, 0)),
-        ("dp", "tensor"),
-    )
+    )
+    sum_qkv_b, sum_up_b = vectors[:2]
+    gain_sum_one, shift_sum_one, gain_sum_two, shift_sum_two, bias_sum = vectors[2:]
     return (
         output,
         grad_input,

time: 356 us -> 223 us (0.63)
  blocking collectives: 143 us -> 6.54 us
  Pallas kernels: 0 us -> 103 us
  waiting for transfers between devices: 66.7 us -> 0.11 us
  starting transfers between devices: 34.5 us -> 0.3 us
  local copies, waits for them, and re-layouts: 17.1 us -> 41.8 us
  other arithmetic: 39.6 us -> 22.6 us
  matrix products: 38.7 us -> 33.2 us
    psum x2 -> x0, blocking collectives: 136 us -> none  [the longest x1 98.5 us: on_device(): sum_qkv_b, sum_up_b = lax.psum((grad_qkv_b, grad_up_b), 'dp')]
    pallas_call x0 -> x1, Pallas kernels: none -> 103 us  [reduce_grads(): pl.pallas_call(functools.partial(reduce_kernel, plan, orders, dp_count, p...]
    all_to_all x4 -> x0, waiting for transfers between devices: 66.5 us -> none  [the longest x1 42.3 us: on_device(): lax.all_to_all(grad_up_w.astype(jnp.bfloat16), 'dp', split_axis=0, concat...]
    all_to_all x4 -> x0, starting transfers between devices: 34.4 us -> none  [the longest x1 10.7 us: on_device(): lax.all_to_all(grad_down_w.astype(jnp.bfloat16), 'dp', split_axis=0, conc...]
    reduce_sum x4 -> x0, other arithmetic: 9.66 us -> none  [the longest x1 2.73 us: on_device(): shard_down = jnp.sum(terms_down, 0)]
    unnamed x79 -> x85, local copies, waits for them, and re-layouts: 3.06 us -> 12 us
    reshape x0 -> x9, local copies, waits for them, and re-layouts: none -> 8.38 us  [the longest x1 2.11 us: on_device(): grad_project.transpose(1, 0, 2).reshape(count, 3 * width)]
    transpose x0 -> x9, local copies, waits for them, and re-layouts: none -> 8.1 us  [the longest x6 4.72 us: place_rows(): rows = rows.transpose([steps - 1 - b for b in order] + [steps, steps + 1])]
  transfers between devices with their start and end apart: 7 -> 3, of which waited for: 2 -> 0; matrix products, arithmetic and copies ran while one was open for 19% -> 16% of each run, Pallas kernels for 0% -> 0%
where the time goes in v1:
time: 223 us; the launch traced here: 222 us
  Pallas kernels  103 us (46%)
  local copies, waits for them, and re-layouts  41.8 us (19%)
  matrix products  33.2 us (15%)
  other arithmetic  22.6 us (10%)
  between operations  14.4 us (6%)
  blocking collectives  6.54 us (3%)
    pallas_call x1, Pallas kernels, reduce_grads(): pl.pallas_call(functools.partial(reduce_kernel, plan, orders, dp_count, p...  103 us
    unnamed x85, local copies, waits for them, and re-layouts  12 us
    dot_general x1, matrix products, on_device(): jnp.einsum('td,fd->tf', back, w_down, preferred_element_type=f32)  5.99 us
    transpose x6, local copies, waits for them, and re-layouts, place_rows(): rows = rows.transpose([steps - 1 - b for b in order] + [steps, steps + 1])  4.72 us
    another operation x3, local copies, waits for them, and re-layouts, on_device(): jnp.stack([unrotary(grad_query, cosine, sine), unrotary(grad_key, cosine,...  4.57 us
  transfers between devices with their start and end apart: 3, of which 0 were waited for; matrix products, arithmetic and copies ran while one was open for 16% of the time, Pallas kernels for 0%

profile of v1, /device:TPU:0, one launch (start us, length us, event | category | flops | bytes accessed | tf_op | source)
XLA Modules:
  0.0 222.1 jit_solution(8269978899558847133)
XLA Ops:
  7.3 1.2 convert_reduce_fusion.4
  8.5 1.1 fusion.57
  10.3 0.7 convert_element_type.130
  11.0 0.7 convert_element_type.120
  12.4 1.8 fusion.48
  14.2 2.2 all_gather.9
  16.4 2.3 %fusion.16 = f32[3,256,384]{2,1,0:T(8,128)S(1)} fusion(bf16[3,768,384]{2,1,0:T(8,128)(2,1)} %param.17, f32[3,384]{1,0:T(4,128)S(1)} %convert_element_type.122, bf16[256,768]{1,0:T(8,128)(2,1)S(1)} %all_gather.9), kind=kOutput, calls=%fused_computation.30 | convolution fusion | flops 453279744 | bytes 3346944 | tf_op jit(solution)/shard_map/td,cde->cte/dot_general | solution.py:315
  18.8 0.9 copy-done.9
  20.2 1.1 slice.214
  22.9 1.1 copy-done.1
  24.8 0.8 copy.84
  25.8 2.1 all_gather.11
  27.9 1.1 convolution_convert_fusion.2
  29.0 1.1 copy.89
  30.1 2.5 %fusion.89 = f32[6,256,256]{1,2,0:T(8,128)} fusion(bf16[256,6,64]{0,2,1:T(8,128)(2,1)S(1)} %bitcast.117, bf16[256,6,64]{0,2,1:T(8,128)(2,1)} %bitcast.137), kind=kOutput, calls=%fused_computation.175 | convolution fusion | flops 50331648 | bytes 1966080 | tf_op jit(solution)/shard_map/qhe,khe->hqk/dot_general | solution.py:351
  32.5 4.4 %fusion.20 = f32[256,6,64]{0,2,1:T(8,128)} fusion(f32[6,256,256]{1,2,0:T(8,128)} %fusion.89, f32[6,256,256]{1,2,0:T(8,128)} %copy-done.1, f32[6,256]{1,0:T(8,128)} %log_add_fusion, bf16[256,6,48]{0,2,1:T(8,128)(2,1)} %copy-done.16, bf16[256,6,16]{0,2,1:T(8,128)(2,1)} %copy-done.23), kind=kOutput, calls=%fused_computation.37 | convolution fusion | flops 53479168 | bytes 3741696 | tf_op jit(solution)/shard_map/hqk,khe->qhe/dot_general | solution.py:354
  37.0 4.4 %fusion.23 = f32[256,6,64]{0,2,1:T(8,128)} fusion(f32[6,256,256]{1,2,0:T(8,128)} %fusion.89, f32[6,256,256]{1,2,0:T(8,128)} %copy-done.1, f32[6,256]{1,0:T(8,128)} %log_add_fusion, bf16[256,6,48]{0,2,1:T(8,128)(2,1)} %copy-done.17, bf16[256,6,16]{0,2,1:T(8,128)(2,1)} %copy-done.22), kind=kOutput, calls=%fused_computation.38 | convolution fusion | flops 53479168 | bytes 3741696 | tf_op jit(solution)/shard_map/hqk,qhe->khe/dot_general | solution.py:355
  41.4 1.0 slice.216
  42.4 1.0 slice_multiply_fusion.3
  43.4 1.6 slice.215
  45.1 2.5 %convolution_convert_fusion.1 = bf16[6,64,256]{2,1,0:T(8,128)(2,1)} fusion(bf16[256,6,64]{0,2,1:T(8,128)(2,1)S(1)} %bitcast.118, f32[6,256,256]{1,2,0:T(8,128)} %copy-done.1, f32[6,256]{1,0:T(8,128)} %log_add_fusion), kind=kOutput, calls=%fused_computation.40 | convolution fusion | flops 51216384 | bytes 1972224 | tf_op jit(solution)/shard_map/hqk,qhe->khe/dot_general | solution.py:356
  47.5 1.6 fusion.70
  49.2 0.7 pad_maximum_fusion.3
  49.8 1.1 copy.93
  50.9 1.6 pad_maximum_fusion.4
  52.5 1.7 copy.94
  54.3 1.7 copy.95
  56.0 3.2 %fusion.18 = bf16[256,768]{1,0:T(8,128)(2,1)} fusion(bf16[3,768,384]{2,1,0:T(8,128)(2,1)} %param.17, bf16[1,256,384]{2,1,0:T(8,128)(2,1)} %copy.95, bf16[1,256,384]{2,1,0:T(8,128)(2,1)} %copy.94, bf16[1,256,384]{2,1,0:T(8,128)(2,1)S(1)} %copy.93), kind=kOutput, calls=%fused_computation.34 | convolution fusion | flops 453771264 | bytes 2752512 | tf_op jit(solution)/shard_map/cte,cde->td/dot_general | solution.py:364
  59.3 2.3 %all_gather.10 = bf16[256,768]{1,0:T(8,128)(2,1)S(1)} all-gather(bf16[128,768]{1,0:T(8,128)(2,1)} %get-tuple-element.41), channel_id=1, replica_groups=mesh['dp'=16,'tensor'=2] {'tensor'}, dimensions={0}, use_global_device_ids=true | all-gather | bytes 589824 | tf_op jit(solution)/shard_map/all_gather | solution.py:308
  61.6 0.7 copy-done.7
  62.3 2.4 %convolution_add_fusion = f32[256,1536]{1,0:T(8,128)S(1)} fusion(bf16[256,768]{1,0:T(8,128)(2,1)S(1)} %all_gather.10, bf16[768,1536]{1,0:T(8,128)(2,1)} %param.21, f32[1536]{0:T(1024)S(1)} %convert_element_type.133), kind=kOutput, calls=%fused_computation.1 | convolution fusion | flops 604372992 | bytes 4331520 | tf_op jit(solution)/shard_map/dot_general | solution.py:331
  64.8 6.0 %convert_reduce_fusion = (f32[1536]{0:T(1024)}, bf16[256,1536]{1,0:T(8,128)(2,1)S(1)}, f32[256,1536]{1,0:T(8,128)}) fusion(f32[256,1536]{1,0:T(8,128)S(1)} %convolution_add_fusion, bf16[256,768]{0,1:T(8,128)(2,1)S(1)} %all_gather.11, bf16[1536,768]{1,0:T(8,128)(2,1)S(1)} %copy-done), kind=kOutput, calls=%fused_computation.4 | convolution fusion | flops 633076224 | bytes 6690816 | tf_op jit(solution)/shard_map/td,fd->tf/dot_general | solution.py:344
  70.8 0.9 copy-done.12
  71.7 1.6 convolution_convert_fusion
  73.6 2.3 %multiply_convert_fusion.1.refs_7_ = bf16[256,1536]{1,0:T(8,128)(2,1)S(1)} fusion(f32[256,1536]{1,0:T(8,128)} %get-tuple-element.31, f32[256,1536]{1,0:T(8,128)} %copy-done.8), kind=kLoop, calls=%fused_computation.10 | loop fusion | flops 1179648 | bytes 3932160 | tf_op jit(solution)/shard_map/convert_element_type | solution.py:332
  76.8 0.8 fusion.88
  77.6 1.1 fusion.19
  78.7 1.1 convert_reduce_fusion.1
  79.9 1.1 fusion.82
  81.0 1.8 copy.106.refs_9_
  82.7 1.1 copy.104
  83.8 2.1 copy.105.refs_8_
  85.9 1.2 copy.96
  87.1 0.8 copy.97
  87.8 0.8 copy.98
  88.6 1.2 copy.101
  89.9 0.8 copy.102
  90.7 0.8 copy.103
  91.4 0.8 copy.99
  92.2 0.8 copy.100
  93.2 1.4 fusion.63
  94.6 1.3 constant_dynamic-update-slice_fusion.3
  95.9 1.3 constant_dynamic-update-slice_fusion.2
  97.2 1.3 constant_dynamic-update-slice_fusion.1
  98.5 1.3 constant_dynamic-update-slice_fusion
  99.9 2.2 convert_reduce_fusion.5
  102.6 1.3 fusion.72.refs_10_
  104.0 103.2 %shard_map.254 = (f32[36,48,128]{2,1,0:T(8,128)}, f32[56,128]{1,0:T(8,128)}) custom-call(bf16[768,256]{1,0:T(8,128)(2,1)} %bitcast.121, bf16[768,256]{1,0:T(8,128)(2,1)} %bitcast.122, bf16[768,256]{1,0:T(8,128)(2,1)} %bitcast.125, bf16[768,256]{1,0:T(8,128)(2,1)} %bitcast.126, bf16[768,256]{1,0:T(8,128)(2,1)} %bitcast.123, bf16[768,256]{1,0:T(8,128)(2,1)} %bitcast.124, ...), custom_call_target="tpu_custom_call" | custom-call | tf_op jit(solution)/shard_map/pallas_call | solution.py:233
  207.2 1.1 slice_bitcast_fusion
  208.3 1.0 slice.145
  209.3 1.5 copy_bitcast_fusion.3
  212.0 0.7 copy.122
  212.7 0.7 copy.123
  213.6 0.8 reshape.273
  (126 shorter events, 9.0 us)
Async XLA Ops:
  7.2 57.6 %copy-start = (bf16[1536,768]{1,0:T(8,128)(2,1)S(1)}, bf16[1536,768]{1,0:T(8,128)(2,1)}, u32[]{:S(2)}) copy-start(bf16[1536,768]{1,0:T(8,128)(2,1)} %param.23) | copy-start | bytes 7077892
  7.2 9.2 %copy-start.34 = (bf16[3,384]{1,0:T(4,128)(2,1)S(1)}, bf16[3,384]{1,0:T(4,128)(2,1)}, u32[]{:S(2)}) copy-start(bf16[3,384]{1,0:T(4,128)(2,1)} %param.18) | copy-start | bytes 6916
  7.2 85.9 %reduce-scatter.6.cloned.1.call-start = ((), (), s32[]{:S(2)}) async-start(), calls=%async_computation.4 | async-start | bytes 589824 | tf_op jit(solution)/shard_map/reduce_scatter | solution.py:366
  8.5 7.9 %copy-start.30 = (f32[128]{0:T(128)}, f32[128]{0:T(128)S(1)}, u32[]{:S(2)}) copy-start(f32[128]{0:T(128)S(1)} %broadcast_multiply_fusion.5) | copy-start | bytes 1540
  9.6 6.7 %copy-start.32 = (f32[128]{0:T(128)}, f32[128]{0:T(128)S(1)}, u32[]{:S(2)}) copy-start(f32[128]{0:T(128)S(1)} %add_rsqrt_fusion) | copy-start | bytes 1540
  10.3 6.0 %copy-start.18 = (f32[768]{0:T(1024)}, f32[768]{0:T(1024)S(1)}, u32[]{:S(2)}) copy-start(f32[768]{0:T(1024)S(1)} %convert_element_type.119) | copy-start | bytes 9220
  11.0 5.4 %copy-start.20 = (f32[768]{0:T(1024)}, f32[768]{0:T(1024)S(1)}, u32[]{:S(2)}) copy-start(f32[768]{0:T(1024)S(1)} %convert_element_type.130) | copy-start | bytes 9220
  16.4 2.3 %copy-start.6 = (bf16[256,768]{1,0:T(8,128)(2,1)}, bf16[256,768]{1,0:T(8,128)(2,1)S(1)}, u32[]{:S(2)}) copy-start(bf16[256,768]{1,0:T(8,128)(2,1)S(1)} %all_gather.9) | copy-start | bytes 1179652
  18.7 1.0 copy-start.9
  19.7 1.5 copy-start.37
  20.1 2.7 %copy-start.16 = (bf16[256,6,48]{0,2,1:T(8,128)(2,1)}, bf16[256,6,48]{0,2,1:T(8,128)(2,1)S(1)}, u32[]{:S(2)}) copy-start(bf16[256,6,48]{0,2,1:T(8,128)(2,1)S(1)} %slice.217) | copy-start | bytes 442372
  20.1 2.7 %copy-start.17 = (bf16[256,6,48]{0,2,1:T(8,128)(2,1)}, bf16[256,6,48]{0,2,1:T(8,128)(2,1)S(1)}, u32[]{:S(2)}) copy-start(bf16[256,6,48]{0,2,1:T(8,128)(2,1)S(1)} %slice.218) | copy-start | bytes 442372
  21.7 0.6 copy-start.15
  21.8 1.1 copy-start.22
  21.8 1.1 copy-start.23
  22.3 3.3 %copy-start.10 = (bf16[128,768]{1,0:T(8,128)(2,1)S(1)}, bf16[128,768]{1,0:T(8,128)(2,1)}, u32[]{:S(2)}) copy-start(bf16[128,768]{1,0:T(8,128)(2,1)} %param.29) | copy-start | bytes 589828
  22.8 1.2 copy-start.1
  22.8 2.0 copy-start.25
  22.8 5.1 %copy-start.5 = (bf16[384,768]{1,0:T(8,128)(2,1)S(1)}, bf16[384,768]{1,0:T(8,128)(2,1)}, u32[]{:S(2)}) copy-start(bf16[384,768]{1,0:T(8,128)(2,1)} %param.19) | copy-start | bytes 1769476
  24.2 0.6 copy-start.27
  56.0 5.5 %copy-start.33 = (bf16[1536]{0:T(1024)(128)(2,1)S(1)}, bf16[1536]{0:T(1024)(128)(2,1)}, u32[]{:S(2)}) copy-start(bf16[1536]{0:T(1024)(128)(2,1)} %param.22) | copy-start | bytes 9220
  59.2 33.9 %reduce-scatter.8.cloned.1.call-start = ((), (), s32[]{:S(2)}) async-start(), calls=%async_computation.5 | async-start | bytes 589824 | tf_op jit(solution)/shard_map/reduce_scatter | solution.py:369
  61.6 0.8 copy-start.7
  64.8 6.0 %copy-start.8 = (f32[256,1536]{1,0:T(8,128)}, f32[256,1536]{1,0:T(8,128)S(1)}, u32[]{:S(2)}) copy-start(f32[256,1536]{1,0:T(8,128)S(1)} %convolution_add_fusion) | copy-start | bytes 4718596
  64.8 6.9 %copy-start.38 = (bf16[768,1536]{1,0:T(8,128)(2,1)S(1)}, bf16[768,1536]{1,0:T(8,128)(2,1)}, u32[]{:S(2)}) copy-start(bf16[768,1536]{1,0:T(8,128)(2,1)} %param.21) | copy-start | bytes 7077892
  70.8 0.9 copy-start.12
  73.3 26.6 %reduce-scatter.4.cloned.1.call-start = ((), (), s32[]{:S(2)}) async-start(), calls=%async_computation.3 | async-start | bytes 589824 | tf_op jit(solution)/shard_map/reduce_scatter | solution.py:333
  73.5 2.4 %copy-start.2 = (f32[6,256,256]{1,2,0:T(8,128)S(1)}, f32[6,256,256]{1,2,0:T(8,128)}, u32[]{:S(2)}) copy-start(f32[6,256,256]{1,2,0:T(8,128)} %copy-done.1) | copy-start | bytes 4718596
  73.5 2.3 %copy-start.13 = (bf16[1,256,384]{1,2,0:T(8,128)(2,1)S(1)}, bf16[1,256,384]{1,2,0:T(8,128)(2,1)}, u32[]{:S(2)}) copy-start(bf16[1,256,384]{1,2,0:T(8,128)(2,1)} %copy.84) | copy-start | bytes 589828
  73.5 2.3 %copy-start.26 = (f32[6,256]{1,0:T(8,128)S(1)}, f32[6,256]{1,0:T(8,128)}, u32[]{:S(2)}) copy-start(f32[6,256]{1,0:T(8,128)} %copy-done.25) | copy-start | bytes 18436
  73.6 2.3 %copy-start.28 = (f32[6,256]{1,0:T(8,128)S(1)}, f32[6,256]{1,0:T(8,128)}, u32[]{:S(2)}) copy-start(f32[6,256]{1,0:T(8,128)} %copy-done.27) | copy-start | bytes 18436
  75.9 0.9 copy-start.4
  76.8 0.8 copy-start.14
  89.8 3.2 %copy-start.31 = (f32[1536]{0:T(1024)S(1)}, f32[1536]{0:T(1024)}, u32[]{:S(2)}) copy-start(f32[1536]{0:T(1024)} %get-tuple-element.29) | copy-start | bytes 18436
  89.8 3.2 %copy-start.35 = (bf16[768]{0:T(1024)(128)(2,1)S(1)}, bf16[768]{0:T(1024)(128)(2,1)}, u32[]{:S(2)}) copy-start(bf16[768]{0:T(1024)(128)(2,1)} %param.24) | copy-start | bytes 4612
  89.8 3.2 %copy-start.36 = (bf16[768]{0:T(1024)(128)(2,1)S(1)}, bf16[768]{0:T(1024)(128)(2,1)}, u32[]{:S(2)}) copy-start(bf16[768]{0:T(1024)(128)(2,1)} %param.20) | copy-start | bytes 4612
  89.8 3.3 %copy-start.3 = (bf16[128,768]{1,0:T(8,128)(2,1)S(1)}, bf16[128,768]{1,0:T(8,128)(2,1)}, u32[]{:S(2)}) copy-start(bf16[128,768]{1,0:T(8,128)(2,1)} %param.15) | copy-start | bytes 589828
  89.8 3.3 %copy-start.19 = (f32[768]{0:T(1024)S(1)}, f32[768]{0:T(1024)}, u32[]{:S(2)}) copy-start(f32[768]{0:T(1024)} %copy-done.18) | copy-start | bytes 9220
  89.9 3.3 %copy-start.21 = (f32[768]{0:T(1024)S(1)}, f32[768]{0:T(1024)}, u32[]{:S(2)}) copy-start(f32[768]{0:T(1024)} %copy-done.20) | copy-start | bytes 9220
  90.7 9.2 %copy-start.11 = (bf16[128,768]{1,0:T(8,128)(2,1)S(1)}, bf16[128,768]{1,0:T(8,128)(2,1)}, u32[]{:S(2)}) copy-start(bf16[128,768]{1,0:T(8,128)(2,1)} %param.29) | copy-start | bytes 589828
  207.2 3.6 %copy-start.24 = (f32[56,128]{1,0:T(8,128)S(1)}, f32[56,128]{1,0:T(8,128)}, u32[]{:S(2)}) copy-start(f32[56,128]{1,0:T(8,128)} %get-tuple-element.17) | copy-start | bytes 86020
  211.4 4.2 %copy-start.29 = (f32[768]{0:T(1024)}, f32[768]{0:T(1024)S(1)}, u32[]{:S(2)}) copy-start(f32[768]{0:T(1024)S(1)} %get-tuple-element.89) | copy-start | bytes 9220
Sparse Core Ops, SparseCore 0:
  59.3 10.3 reduce-scatter.5
  73.4 10.3 reduce-scatter.7
  86.1 8.9 reduce-scatter.3

commit v2 on v1

--- a/solution.py
+++ b/solution.py
@@ -10,7 +10,7 @@
 
 MESH = pl.DeviceIdType.MESH
 WIDE = 128
-LAG = 2
+LAG = 4
 ROWS_DP = 24
 ROWS_ALL = 32
 
@@ -79,7 +79,8 @@
 def bit_orders(steps):
     plain = list(range(steps))
     other = [1, 0] + plain[2:] if steps > 1 else plain
-    return plain, other
+    far = plain[2:] + plain[:2]
+    return plain, other, far
 
 
 def place_rows(left, dp_count, share, padded, order):
@@ -94,11 +95,13 @@
 
 
 def reduce_kernel(plan, orders, dp_count, padded, *refs):
-    lefts, rights = refs[:6], refs[6:10]
-    vec_ref, out_ref, vec_out = refs[10:13]
-    grid, landed, vec_acc, vec_got = refs[13:17]
-    send_sem, recv_sem, vec_send, vec_recv = refs[17:]
+    lefts, rights = refs[:3], refs[3:7]
+    vec_ref, out_ref, vec_out = refs[7:10]
+    grid, landed, vec_acc, vec_got = refs[10:14]
+    send_sem, recv_sem, vec_send, vec_recv = refs[14:]
     steps = len(orders[0])
+    by_array = sorted(range(len(plan)), key=lambda chunk: plan[chunk][1:])
+    slots = {chunk: slot for slot, chunk in enumerate(by_array)}
     me = lax.axis_index("dp")
     side = lax.axis_index("tensor")
     bits = [(me // (1 << b)) % 2 for b in range(steps)]
@@ -111,14 +114,14 @@
     pl.semaphore_wait(barrier, steps + 1)
 
     def span(chunk, step):
-        order = orders[chunk % 2]
+        order = orders[plan[chunk][0]]
         start = 0
         for s in range(step):
             start = start + bits[order[s]] * ((dp_count >> (s + 1)) * padded)
         return start, (dp_count >> (step + 1)) * padded
 
     def copy(chunk, step):
-        order = orders[chunk % 2]
+        order = orders[plan[chunk][0]]
         start, half = span(chunk, step)
         away = pl.multiple_of(start + (1 - bits[order[step]]) * half, 16)
         offset = (dp_count - (dp_count >> step)) * padded
@@ -132,7 +135,7 @@
         )
 
     def absorb(chunk, step):
-        order = orders[chunk % 2]
+        order = orders[plan[chunk][0]]
         start, half = span(chunk, step)
         copy(chunk, step).wait_recv()
         keep = pl.ds(pl.multiple_of(start + bits[order[step]] * half, 16), half)
@@ -141,14 +144,14 @@
             jnp.float32
         )
         if step == steps - 1:
-            out_ref[chunk] = total
+            out_ref[slots[chunk]] = total
         else:
             grid[chunk, keep] = total.astype(jnp.bfloat16)
 
     def produce(chunk):
         which, right, column = plan[chunk]
         grid[chunk] = jnp.dot(
-            lefts[2 * which + chunk % 2][...],
+            lefts[which][...],
             rights[right][:, pl.ds(column, WIDE)],
             preferred_element_type=jnp.float32,
         ).astype(jnp.bfloat16)
@@ -212,14 +215,15 @@
     padded = -(-share // 16) * 16
     orders = bit_orders(steps)
     lefts = [
-        place_rows(left, dp_count, share, padded, order)
-        for left in (second, back, first)
-        for order in orders
+        place_rows(left, dp_count, share, padded, orders[which])
+        for which, left in enumerate((second, back, first))
     ]
     rights = (grad_inner, active, grad_project, mixed)
     plan = []
     for which, right in ((0, 0), (1, 1), (2, 2), (1, 3)):
-        plan += [(which, right, c) for c in range(0, rights[right].shape[1], WIDE)]
+        columns = range(0, rights[right].shape[1], WIDE)
+        plan += [((i + 0.5) / len(columns), which, right, c) for i, c in enumerate(columns)]
+    plan = [entry[1:] for entry in sorted(plan)]
     flat_dp = jnp.concatenate([v.reshape(-1) for v in vec_dp])
     flat_all = jnp.concatenate([v.reshape(-1) for v in vec_all])
     vec = jnp.concatenate(
@@ -236,7 +240,7 @@
             jax.ShapeDtypeStruct((chunks, padded, WIDE), f32),
             jax.ShapeDtypeStruct((ROWS_DP + ROWS_ALL, 128), f32),
         ),
-        in_specs=[whole] * 11,
+        in_specs=[whole] * 8,
         out_specs=(whole, whole),
         scratch_shapes=[
             pltpu.VMEM((chunks, dp_count * padded, WIDE), bf16),
@@ -278,6 +282,16 @@
     return shard_up, shard_down, shard_qkv, shard_dense, results
 
 
+def pair_sum(part):
+    mine = lax.axis_index("tensor")
+    part = part.astype(jnp.bfloat16)
+    half = part.shape[0] // 2
+    away = lax.dynamic_slice_in_dim(part, (1 - mine) * half, half, 0)
+    kept = lax.dynamic_slice_in_dim(part, mine * half, half, 0)
+    got = lax.ppermute(away, "tensor", [(0, 1), (1, 0)])
+    return kept.astype(jnp.float32) + got.astype(jnp.float32)
+
+
 def on_device(
     tokens,
     bounds,
@@ -330,15 +344,10 @@
     mixed = mixed.astype(bf16).reshape(count, width)
     inner = jnp.dot(second, w_up, preferred_element_type=f32) + b_up.astype(f32)
     active = gelu_exact(inner).astype(bf16)
-    summed = lax.psum_scatter(
-        (
-            jnp.dot(mixed, w_dense, preferred_element_type=f32)
-            + jnp.dot(active, w_down, preferred_element_type=f32)
-        ).astype(jnp.bfloat16),
-        "tensor",
-        scatter_dimension=0,
-        tiled=True,
-    ).astype(jnp.float32)
+    summed = pair_sum(
+        jnp.dot(mixed, w_dense, preferred_element_type=f32)
+        + jnp.dot(active, w_down, preferred_element_type=f32)
+    )
     output = (rows + summed + (b_dense.astype(f32) + b_down.astype(f32))).astype(bf16)
     back = lax.all_gather(cotangent, "tensor", axis=0, tiled=True)
     grad_active = jnp.einsum("td,fd->tf", back, w_down, preferred_element_type=f32)
@@ -362,14 +371,8 @@
     grad_project = grad_project.reshape(3, count, width).astype(bf16)
     grad_qkv_b = jnp.sum(grad_project.astype(f32), 1)
     part_first = jnp.einsum("cte,cde->td", grad_project, w_qkv, preferred_element_type=f32)
-    grad_first, grad_second = (
-        lax.psum_scatter(
-            part_first.astype(jnp.bfloat16), "tensor", scatter_dimension=0, tiled=True
-        ).astype(jnp.float32),
-        lax.psum_scatter(
-            part_second.astype(jnp.bfloat16), "tensor", scatter_dimension=0, tiled=True
-        ).astype(jnp.float32),
-    )
+    grad_first = pair_sum(part_first)
+    grad_second = pair_sum(part_second)
     back_own = cotangent.astype(f32)
     into_one, gain_grad_one, shift_grad_one = norm_back(
         grad_first, normal_one, scaler_one, gain_one

time: 223 us -> 194 us (0.87)
  Pallas kernels: 103 us -> 75.6 us
  between operations: 14.4 us -> 1.12 us
  local copies, waits for them, and re-layouts: 41.8 us -> 51.2 us
  other arithmetic: 22.6 us -> 29.5 us
  matrix products: 33.2 us -> 27.8 us
    pallas_call x1, Pallas kernels: 103 us -> 75.6 us  [reduce_grads(): pl.pallas_call(functools.partial(reduce_kernel, plan, orders, dp_count, p...]
    slice x2, local copies, waits for them, and re-layouts: 0.03 us -> 3.35 us  [rotary(): v[..., ROT:]]
    unnamed x85 -> x91, local copies, waits for them, and re-layouts: 12 us -> 9.58 us
    transpose x6 -> x3, local copies, waits for them, and re-layouts: 4.72 us -> 4.34 us  [place_rows(): rows = rows.transpose([steps - 1 - b for b in order] + [steps, steps + 1])]
  transfers between devices with their start and end apart: 3 -> 3, of which waited for: 0 -> 0; matrix products, arithmetic and copies ran while one was open for 16% -> 19% of each run, Pallas kernels for 0% -> 0%
where the time goes in v2:
time: 194 us; the launch traced here: 193 us
  Pallas kernels  75.6 us (39%)
  local copies, waits for them, and re-layouts  51.2 us (26%)
  other arithmetic  29.5 us (15%)
  matrix products  27.8 us (14%)
  blocking collectives  6.54 us (3%)
    pallas_call x1, Pallas kernels, reduce_grads(): pl.pallas_call(functools.partial(reduce_kernel, plan, orders, dp_count, p...  75.6 us
    unnamed x91, local copies, waits for them, and re-layouts  9.58 us
    dot_general x1, matrix products, on_device(): jnp.einsum('td,fd->tf', back, w_down, preferred_element_type=f32)  5.75 us
    another operation x3, local copies, waits for them, and re-layouts, on_device(): jnp.stack([unrotary(grad_query, cosine, sine), unrotary(grad_key, cosine,...  4.57 us
    dot_general x1, matrix products, on_device(): jnp.einsum('hqk,khe->qhe', grad_raw, key, preferred_element_type=f32)  4.48 us
    dot_general x1, matrix products, on_device(): jnp.einsum('hqk,qhe->khe', grad_raw, query, preferred_element_type=f32)  4.39 us
    transpose x3, local copies, waits for them, and re-layouts, place_rows(): rows = rows.transpose([steps - 1 - b for b in order] + [steps, steps + 1])  4.34 us
  transfers between devices with their start and end apart: 3, of which 0 were waited for; matrix products, arithmetic and copies ran while one was open for 19% of the time, Pallas kernels for 0%

profile of v2, /device:TPU:0, one launch (start us, length us, event | category | flops | bytes accessed | tf_op | source)
XLA Modules:
  0.0 192.5 jit_solution(13509991893593528877)
XLA Ops:
  0.7 1.2 convert_reduce_fusion.2
  1.9 1.1 fusion.59
  6.5 1.8 fusion.46
  8.3 2.2 %all_gather.9 = bf16[256,768]{1,0:T(8,128)(2,1)S(1)} all-gather(bf16[128,768]{1,0:T(8,128)(2,1)S(1)} %get-tuple-element.41), channel_id=1, replica_groups=mesh['dp'=16,'tensor'=2] {'tensor'}, dimensions={0}, use_global_device_ids=true | all-gather | bytes 589824 | tf_op jit(solution)/shard_map/all_gather | solution.py:321
  10.5 2.3 %fusion.16 = f32[3,256,384]{2,1,0:T(8,128)S(1)} fusion(bf16[3,768,384]{2,1,0:T(8,128)(2,1)} %param.17, f32[3,384]{1,0:T(4,128)S(1)} %convert_element_type.131, bf16[256,768]{1,0:T(8,128)(2,1)S(1)} %all_gather.9), kind=kOutput, calls=%fused_computation.30 | convolution fusion | flops 453279744 | bytes 3346944 | tf_op jit(solution)/shard_map/td,cde->cte/dot_general | solution.py:329
  13.6 0.9 copy.79
  14.5 1.7 slice.218
  16.2 0.9 copy.80
  17.1 1.6 slice.217
  18.8 1.6 slice_negate_fusion.2
  22.0 0.8 copy.82
  22.9 2.3 %all_gather.11 = bf16[256,768]{0,1:T(8,128)(2,1)S(1)} all-gather(bf16[128,768]{0,1:T(8,128)(2,1)} %copy.82), channel_id=1, replica_groups=mesh['dp'=16,'tensor'=2] {'tensor'}, dimensions={0}, use_global_device_ids=true | all-gather | bytes 589824 | tf_op jit(solution)/shard_map/all_gather | solution.py:352
  25.1 1.1 convolution_convert_fusion.2
  26.2 1.1 copy.83
  27.3 1.7 copy.78
  29.0 1.1 fusion.73
  30.2 1.5 fusion.91
  31.9 1.1 convolution_convert_fusion.1
  33.0 1.6 fusion.93
  34.6 4.5 %fusion.20 = f32[256,6,64]{0,2,1:T(8,128)} fusion(f32[6,256,256]{1,2,0:T(8,128)} %fusion.93, f32[6,256,256]{1,2,0:T(8,128)} %copy-done.1, f32[6,256]{1,0:T(8,128)} %copy-done.33, bf16[256,6,48]{0,2,1:T(8,128)(2,1)} %slice.217, bf16[256,6,16]{0,2,1:T(8,128)(2,1)} %copy-done.28), kind=kOutput, calls=%fused_computation.37 | convolution fusion | flops 53479168 | bytes 3741696 | tf_op jit(solution)/shard_map/hqk,khe->qhe/dot_general | solution.py:363
  39.1 4.4 %fusion.23 = f32[256,6,64]{0,2,1:T(8,128)} fusion(f32[6,256,256]{1,2,0:T(8,128)} %fusion.93, f32[6,256,256]{1,2,0:T(8,128)} %copy-done.1, f32[6,256]{1,0:T(8,128)S(1)} %copy-done.34, bf16[256,6,48]{0,2,1:T(8,128)(2,1)S(1)} %copy-done.22, bf16[256,6,16]{0,2,1:T(8,128)(2,1)} %copy-done.27), kind=kOutput, calls=%fused_computation.38 | convolution fusion | flops 53479168 | bytes 3741696 | tf_op jit(solution)/shard_map/hqk,qhe->khe/dot_general | solution.py:364
  43.5 1.6 slice.215
  45.1 1.6 slice.216
  46.8 1.6 slice_multiply_fusion.3
  48.4 1.1 copy.89
  49.5 0.9 fusion.89
  50.4 0.8 fusion.90
  51.2 1.6 fusion.74
  52.8 1.6 pad_maximum_fusion.3
  54.4 1.7 copy.87
  56.2 1.6 pad_maximum_fusion.4
  57.8 1.7 copy.88
  59.5 2.5 %fusion.18 = bf16[256,768]{1,0:T(8,128)(2,1)S(1)} fusion(bf16[3,768,384]{2,1,0:T(8,128)(2,1)} %param.17, bf16[1,256,384]{2,1,0:T(8,128)(2,1)S(1)} %copy.89, bf16[1,256,384]{2,1,0:T(8,128)(2,1)} %copy.88, bf16[1,256,384]{2,1,0:T(8,128)(2,1)} %copy.87), kind=kOutput, calls=%fused_computation.34 | convolution fusion | flops 453771264 | bytes 2752512 | tf_op jit(solution)/shard_map/cte,cde->td/dot_general | solution.py:373
  62.1 0.8 constant_dynamic-slice_fusion.1
  63.2 2.1 %all_gather.10 = bf16[256,768]{1,0:T(8,128)(2,1)S(1)} all-gather(bf16[128,768]{1,0:T(8,128)(2,1)S(1)} %copy-done.17), channel_id=1, replica_groups=mesh['dp'=16,'tensor'=2] {'tensor'}, dimensions={0}, use_global_device_ids=true | all-gather | bytes 589824 | tf_op jit(solution)/shard_map/all_gather | solution.py:322
  65.3 0.8 copy-done.8
  66.1 0.8 convolution_add_fusion
  66.9 5.7 %convert_reduce_fusion = (f32[1536]{0:T(1024)}, bf16[256,1536]{1,0:T(8,128)(2,1)S(1)}, f32[256,1536]{1,0:T(8,128)S(1)}) fusion(f32[256,1536]{1,0:T(8,128)S(1)} %convolution_add_fusion, bf16[256,768]{0,1:T(8,128)(2,1)S(1)} %all_gather.11, bf16[1536,768]{1,0:T(8,128)(2,1)S(1)} %copy-done), kind=kOutput, calls=%fused_computation.4 | convolution fusion | flops 633076224 | bytes 6690816 | tf_op jit(solution)/shard_map/td,fd->tf/dot_general | solution.py:353
  72.6 0.8 convolution_convert_fusion
  75.1 0.8 fusion.92
  76.4 0.8 copy-done.9
  78.2 1.7 copy.97.refs_6_
  80.0 1.7 convert_reduce_fusion.1
  81.7 1.2 fusion.86
  82.9 1.9 copy.90
  84.8 1.8 copy.91
  86.6 1.9 copy.93
  88.5 1.8 copy.94
  90.3 0.8 copy.92
  91.8 1.1 copy.95
  92.8 2.2 %copy.96.refs_5_ = bf16[256,1152]{1,0:T(8,128)(2,1)} copy(bf16[256,1152]{0,1:T(8,128)(2,1)} %bitcast.102) | data formatting | bytes 1179648 | tf_op jit(solution)/shard_map/reshape | solution.py:388
  96.5 1.7 fusion.57
  98.2 1.3 constant_dynamic-update-slice_fusion.3
  99.5 1.3 constant_dynamic-update-slice_fusion.2
  100.8 1.3 constant_dynamic-update-slice_fusion.1
  102.1 1.3 constant_dynamic-update-slice_fusion
  103.4 2.4 %convert_reduce_fusion.3 = (f32[768]{0:T(1024)S(1)}, bf16[128,768]{1,0:T(8,128)(2,1)}, bf16[128,768]{1,0:T(8,128)(2,1)}) fusion(bf16[128,768]{1,0:T(8,128)(2,1)S(1)} %copy-done.15, f32[128]{0:T(128)S(1)} %broadcast_multiply_fusion.1, f32[128]{0:T(128)S(1)} %broadcast_multiply_fusion.2, f32[768]{0:T(1024)S(1)} %copy-done.26, ...), kind=kLoop, calls=%fused_computation.53 | loop fusion | flops 2948352 | bytes 1981444 | tf_op jit(solution)/shard_map/reduce_sum | solution.py:393
  106.4 75.6 %shard_map.254 = (f32[36,48,128]{2,1,0:T(8,128)}, f32[56,128]{1,0:T(8,128)}) custom-call(bf16[768,256]{1,0:T(8,128)(2,1)} %bitcast.109, bf16[768,256]{1,0:T(8,128)(2,1)} %bitcast.111, bf16[768,256]{1,0:T(8,128)(2,1)} %bitcast.110, bf16[256,1536]{1,0:T(8,128)(2,1)} %copy-done.16, bf16[256,1536]{1,0:T(8,128)(2,1)} %copy-done.4, ...), custom_call_target="tpu_custom_call" | custom-call | tf_op jit(solution)/shard_map/pallas_call | solution.py:237
  182.0 1.3 slice_bitcast_fusion.3
  184.0 1.4 slice_bitcast_fusion.4
  185.4 1.5 copy_bitcast_fusion.3
  186.9 0.9 slice.145
  187.8 1.1 slice_bitcast_fusion
  190.4 0.8 reshape.261
  (129 shorter events, 16.1 us)
Async XLA Ops:
  0.6 66.2 %copy-start = (bf16[1536,768]{1,0:T(8,128)(2,1)S(1)}, bf16[1536,768]{1,0:T(8,128)(2,1)}, u32[]{:S(2)}) copy-start(bf16[1536,768]{1,0:T(8,128)(2,1)} %param.23) | copy-start | bytes 7077892
  1.9 6.4 %copy-start.37 = (f32[128]{0:T(128)}, f32[128]{0:T(128)S(1)}, u32[]{:S(2)}) copy-start(f32[128]{0:T(128)S(1)} %broadcast_multiply_fusion.5) | copy-start | bytes 1540
  3.0 5.3 %copy-start.38 = (f32[128]{0:T(128)}, f32[128]{0:T(128)S(1)}, u32[]{:S(2)}) copy-start(f32[128]{0:T(128)S(1)} %add_rsqrt_fusion) | copy-start | bytes 1540
  3.7 4.6 %copy-start.23 = (f32[768]{0:T(1024)}, f32[768]{0:T(1024)S(1)}, u32[]{:S(2)}) copy-start(f32[768]{0:T(1024)S(1)} %convert_element_type.128) | copy-start | bytes 9220
  4.4 3.9 %copy-start.25 = (f32[768]{0:T(1024)}, f32[768]{0:T(1024)S(1)}, u32[]{:S(2)}) copy-start(f32[768]{0:T(1024)S(1)} %convert_element_type.139) | copy-start | bytes 9220
  10.5 2.3 %copy-start.7 = (bf16[256,768]{1,0:T(8,128)(2,1)}, bf16[256,768]{1,0:T(8,128)(2,1)S(1)}, u32[]{:S(2)}) copy-start(bf16[256,768]{1,0:T(8,128)(2,1)S(1)} %all_gather.9) | copy-start | bytes 1179652
  13.6 6.8 %copy-start.40 = (s32[1,5]{1,0:T(1,128)S(1)}, s32[1,5]{1,0:T(1,128)}, u32[]{:S(2)}) copy-start(s32[1,5]{1,0:T(1,128)} %param.16) | copy-start | bytes 64
  13.6 8.5 %copy-start.14 = (bf16[128,768]{1,0:T(8,128)(2,1)S(1)}, bf16[128,768]{1,0:T(8,128)(2,1)}, u32[]{:S(2)}) copy-start(bf16[128,768]{1,0:T(8,128)(2,1)} %param.29) | copy-start | bytes 589828
  14.5 10.7 %copy-start.5 = (bf16[384,768]{1,0:T(8,128)(2,1)S(1)}, bf16[384,768]{1,0:T(8,128)(2,1)}, u32[]{:S(2)}) copy-start(bf16[384,768]{1,0:T(8,128)(2,1)} %param.19) | copy-start | bytes 1769476
  30.1 1.5 copy-start.27
  30.1 1.5 copy-start.28
  31.6 1.4 copy-start.1
  31.6 1.4 copy-start.29
  31.7 1.4 copy-start.18
  31.9 1.1 copy-start.31
  31.9 1.1 copy-start.33
  34.6 4.5 %copy-start.22 = (bf16[256,6,48]{0,2,1:T(8,128)(2,1)S(1)}, bf16[256,6,48]{0,2,1:T(8,128)(2,1)}, u32[]{:S(2)}) copy-start(bf16[256,6,48]{0,2,1:T(8,128)(2,1)} %slice.218) | copy-start | bytes 442372
  34.6 4.5 %copy-start.34 = (f32[6,256]{1,0:T(8,128)S(1)}, f32[6,256]{1,0:T(8,128)}, u32[]{:S(2)}) copy-start(f32[6,256]{1,0:T(8,128)} %copy-done.33) | copy-start | bytes 18436
  39.1 7.7 %copy-start.21 = (f32[256,16]{0,1:T(8,128)S(1)}, f32[256,16]{0,1:T(8,128)}, u32[]{:S(2)}) copy-start(f32[256,16]{0,1:T(8,128)} %get-tuple-element.62) | copy-start | bytes 49156
  49.5 30.5 %copy-start.6 = (bf16[1,256,384]{2,1,0:T(8,128)(2,1)}, bf16[1,256,384]{2,1,0:T(8,128)(2,1)S(1)}, u32[]{:S(2)}) copy-start(bf16[1,256,384]{2,1,0:T(8,128)(2,1)S(1)} %copy.89) | copy-start | bytes 589828
  59.5 3.7 %copy-start.39 = (bf16[1536]{0:T(1024)(128)(2,1)S(1)}, bf16[1536]{0:T(1024)(128)(2,1)}, u32[]{:S(2)}) copy-start(bf16[1536]{0:T(1024)(128)(2,1)} %param.22) | copy-start | bytes 9220
  59.5 3.7 %copy-start.17 = (bf16[128,768]{1,0:T(8,128)(2,1)S(1)}, bf16[128,768]{1,0:T(8,128)(2,1)}, u32[]{:S(2)}) copy-start(bf16[128,768]{1,0:T(8,128)(2,1)} %get-tuple-element.42) | copy-start | bytes 589828
  59.5 6.6 %copy-start.41 = (bf16[768,1536]{1,0:T(8,128)(2,1)S(1)}, bf16[768,1536]{1,0:T(8,128)(2,1)}, u32[]{:S(2)}) copy-start(bf16[768,1536]{1,0:T(8,128)(2,1)} %param.21) | copy-start | bytes 7077892
  62.1 3.2 %copy-start.11 = (bf16[256,768]{1,0:T(8,128)(2,1)}, bf16[256,768]{1,0:T(8,128)(2,1)S(1)}, u32[]{:S(2)}) copy-start(bf16[256,768]{1,0:T(8,128)(2,1)S(1)} %fusion.18) | copy-start | bytes 1179652
  62.9 33.6 %collective-permute-start.1 = (bf16[128,768]{1,0:T(8,128)(2,1)}, bf16[128,768]{1,0:T(8,128)(2,1)}, u32[]{:S(2)}, u32[]{:S(2)}) collective-permute-start(bf16[128,768]{1,0:T(8,128)(2,1)} %constant_dynamic-slice_fusion.1), channel_id=1, source_target_pairs={{0,1},{1,0},{2,3},{3,2},{4,5},{5,4},{6,7},{7,6},{8,9},{9,8},{10,11... | collective-permute-start | bytes 589832 | tf_op jit(solution)/shard_map/ppermute | solution.py:291
  65.3 0.8 copy-start.8
  72.6 0.9 copy-start.16
  72.6 1.8 copy-start.2
  72.6 1.8 copy-start.19
  72.6 1.8 copy-start.30
  72.6 1.8 copy-start.32
  73.5 1.3 copy-start.13
  74.3 22.2 %collective-permute-start.2 = (bf16[128,768]{1,0:T(8,128)(2,1)}, bf16[128,768]{1,0:T(8,128)(2,1)}, u32[]{:S(2)}, u32[]{:S(2)}) collective-permute-start(bf16[128,768]{1,0:T(8,128)(2,1)} %constant_dynamic-slice_fusion), channel_id=1, source_target_pairs={{0,1},{1,0},{2,3},{3,2},{4,5},{5,4},{6,7},{7,6},{8,9},{9,8},{10,11... | collective-permute-start | bytes 589832 | tf_op jit(solution)/shard_map/ppermute | solution.py:291
  74.8 1.2 copy-start.20
  75.1 0.9 copy-start.4
  76.4 0.8 copy-start.9
  77.9 25.5 %collective-permute-start = (bf16[128,768]{1,0:T(8,128)(2,1)}, bf16[128,768]{1,0:T(8,128)(2,1)}, u32[]{:S(2)}, u32[]{:S(2)}) collective-permute-start(bf16[128,768]{1,0:T(8,128)(2,1)} %constant_dynamic-slice_fusion.2), channel_id=1, source_target_pairs={{0,1},{1,0},{2,3},{3,2},{4,5},{5,4},{6,7},{7,6},{8,9},{9,8},{10,11... | collective-permute-start | bytes 589832 | tf_op jit(solution)/shard_map/ppermute | solution.py:291
  90.3 6.2 %copy-start.3 = (bf16[128,768]{1,0:T(8,128)(2,1)S(1)}, bf16[128,768]{1,0:T(8,128)(2,1)}, u32[]{:S(2)}) copy-start(bf16[128,768]{1,0:T(8,128)(2,1)} %param.15) | copy-start | bytes 589828
  90.3 6.2 %copy-start.24 = (f32[768]{0:T(1024)S(1)}, f32[768]{0:T(1024)}, u32[]{:S(2)}) copy-start(f32[768]{0:T(1024)} %copy-done.23) | copy-start | bytes 9220
  90.3 6.2 %copy-start.26 = (f32[768]{0:T(1024)S(1)}, f32[768]{0:T(1024)}, u32[]{:S(2)}) copy-start(f32[768]{0:T(1024)} %copy-done.25) | copy-start | bytes 9220
  91.8 11.7 %copy-start.10 = (bf16[256,768]{1,0:T(8,128)(2,1)S(1)}, bf16[256,768]{1,0:T(8,128)(2,1)}, u32[]{:S(2)}) copy-start(bf16[256,768]{1,0:T(8,128)(2,1)} %copy-done.9) | copy-start | bytes 1179652
  92.8 10.6 %copy-start.12 = (bf16[256,768]{1,0:T(8,128)(2,1)S(1)}, bf16[256,768]{1,0:T(8,128)(2,1)}, u32[]{:S(2)}) copy-start(bf16[256,768]{1,0:T(8,128)(2,1)} %copy-done.11) | copy-start | bytes 1179652
  92.8 10.6 %copy-start.15 = (bf16[128,768]{1,0:T(8,128)(2,1)S(1)}, bf16[128,768]{1,0:T(8,128)(2,1)}, u32[]{:S(2)}) copy-start(bf16[128,768]{1,0:T(8,128)(2,1)} %param.29) | copy-start | bytes 589828
  103.4 2.4 %copy-start.35 = (f32[3840]{0:T(1024)S(1)}, f32[3840]{0:T(1024)}, u32[]{:S(2)}) copy-start(f32[3840]{0:T(1024)} %constant_dynamic-update-slice_fusion) | copy-start | bytes 46084
  185.4 6.6 %copy-start.36 = (f32[768]{0:T(1024)}, f32[768]{0:T(1024)S(1)}, u32[]{:S(2)}) copy-start(f32[768]{0:T(1024)S(1)} %get-tuple-element.90) | copy-start | bytes 9220
